TPU v7x, 256 devices: a whole 4x4x8 slice. The times are simulated.
256 devices in a mesh: section: 8 (over x, core), vocab: 32 (over y, z).
Axes of the slice: x: 4, y: 4, z: 8, core: 2. Of those that a mesh axis runs over, the one named last changes fastest.
Arguments:
- hidden: bfloat16 [2048, 8192], P('section', 'vocab'), may hold values from -1000 to 1000
- norm_gain: float32 [8192], P('vocab'), may hold values from 0.5 to 1.5
- head_weight: bfloat16 [8192, 98304], P(None, ('section', 'vocab')), may hold values from -5 to 5
- exit_mask: int32 [2048], replicated, may hold values from 0 to 1, as said below
- targets: int32 [2048], replicated, may hold values from 0 to 98303
- section_weight: float32 [8], replicated, may hold values from 8 to 24
Outputs:
- mean_loss: float32 [], replicated
- d_hidden: bfloat16 [2048, 8192], P('section', 'vocab')
- d_gain: float32 [8192], P('vocab')
- d_head: bfloat16 [8192, 98304], P(None, ('section', 'vocab'))
Inputs may be any that keep to these rules, and one draw needn't show every extreme that they name: `exit_mask`: exactly 384 ones in all; at most 96 ones among the 256 tokens of one section group, and exactly 96 in some section group.
All inputs are finite; a program needn't handle non-finite values.
Results may differ from a plain program's by a relative error of at most 0.027.
Values may be sent and summed in bfloat16 or wider, within the bound.
No kernel may reach another device: no remote copies, remote signals or barrier semaphores. Data moves between devices by JAX's collectives and lax.ppermute only.
A program may use at most 128 MiB of HBM per device.

v0:
```python
import jax
import jax.numpy as jnp
from jax import lax
from jax.sharding import PartitionSpec as P

D = 8192
CAP = 96
EXIT_MEAN = 48
epsilon = 1e-05


def body(hidden, norm_gain, head_weight, exit_mask, targets, section_weight):
    section_count = lax.axis_size("section")
    vocab_count = lax.axis_size("vocab")
    section_index = lax.axis_index("section")
    vocab_index = lax.axis_index("vocab")
    token_count = hidden.shape[0]
    vocab_width = head_weight.shape[1]
    exit_total = EXIT_MEAN * section_count
    mask_grid = exit_mask.reshape(section_count, token_count)
    rank_grid = jnp.cumsum(mask_grid, axis=1) - 1
    slot_iota = jnp.arange(CAP, dtype=jnp.int32)
    token_iota = jnp.arange(token_count, dtype=jnp.int32)
    slot_hit = (rank_grid[:, None, :] == slot_iota[None, :, None]) & (mask_grid[:, None, :] == 1)
    own_hit = lax.dynamic_index_in_dim(slot_hit, section_index, 0, keepdims=False)
    rows_own = jnp.dot(own_hit.astype(jnp.bfloat16), hidden, preferred_element_type=jnp.float32)
    squares = lax.psum(jnp.sum(rows_own * rows_own, axis=1), "vocab")
    inverse = lax.rsqrt(squares / D + epsilon)
    normed_own = (rows_own * inverse[:, None] * norm_gain[None, :]).astype(jnp.bfloat16)
    section_rows = lax.all_gather(normed_own, "section", axis=0, tiled=True)
    local_place = jnp.sum(jnp.where(slot_hit, token_iota[None, None, :], 0), axis=2)
    section_start = jnp.arange(section_count, dtype=jnp.int32)[:, None] * token_count
    positions = (local_place + section_start).reshape(-1)
    live_rows = jnp.any(slot_hit, axis=2).reshape(-1).astype(jnp.float32)
    full_rows = lax.all_gather(section_rows, "vocab", axis=1, tiled=True)
    labels = targets[positions]
    weights = section_weight[positions // token_count] * live_rows
    logits = jnp.dot(full_rows, head_weight, preferred_element_type=jnp.float32)
    vocab_start = (section_index * vocab_count + vocab_index) * vocab_width
    column = jnp.arange(vocab_width, dtype=jnp.int32) + vocab_start
    onehot = (column[None, :] == labels[:, None]).astype(jnp.float32)
    picked_part = jnp.sum(logits * onehot, axis=1)
    local_peak = jnp.max(logits, axis=1)
    row_peak = lax.pmax(local_peak, ("section", "vocab"))
    local_total = jnp.sum(jnp.exp(logits - row_peak[:, None]), axis=1)
    row_total, picked = lax.psum((local_total, picked_part), ("section", "vocab"))
    logsum = row_peak + jnp.log(row_total)
    mean_loss = jnp.sum(live_rows * (logsum - picked)) / exit_total
    softmax_rows = jnp.exp(logits - logsum[:, None])
    dlogits = (weights[:, None] * (softmax_rows - onehot)).astype(jnp.bfloat16)
    d_head = lax.dot_general(
        full_rows, dlogits, (((0,), (0,)), ((), ())), preferred_element_type=jnp.float32
    ).astype(jnp.bfloat16)
    grads_turned = lax.psum_scatter(
        lax.dot_general(
            head_weight, dlogits, (((1,), (1,)), ((), ())), preferred_element_type=jnp.float32
        ).astype(jnp.bfloat16),
        "vocab",
        scatter_dimension=0,
        tiled=True,
    )
    own_grads = lax.psum_scatter(grads_turned, "section", scatter_dimension=1, tiled=True).astype(
        jnp.float32
    )
    d_normed = own_grads.T
    scaled = d_normed * norm_gain[None, :]
    inner_dots = lax.psum(jnp.sum(scaled * rows_own, axis=1), "vocab") / D
    d_rows = (
        inverse[:, None] * scaled - rows_own * (inverse * inverse * inverse * inner_dots)[:, None]
    )
    gain_part = jnp.sum(d_normed * rows_own * inverse[:, None], axis=0)
    d_gain = lax.psum(gain_part, "section")
    d_hidden = lax.dot_general(
        own_hit.astype(jnp.float32),
        d_rows,
        (((0,), (0,)), ((), ())),
        precision=lax.Precision.HIGHEST,
        preferred_element_type=jnp.float32,
    ).astype(jnp.bfloat16)
    return (mean_loss, d_hidden, d_gain, d_head)


def solution(mesh):
    placed = (P("section", "vocab"), P("vocab"), P(None, ("section", "vocab")), P(), P(), P())
    return jax.shard_map(
        body,
        mesh=mesh,
        in_specs=placed,
        out_specs=(P(), P("section", "vocab"), P("vocab"), P(None, ("section", "vocab"))),
        check_vma=False,
    )
```

profile of v0, /device:TPU:0, one launch (start us, length us, event | category | flops | bytes accessed | tf_op | source)
XLA Modules:
  0.0 760.4 jit_solution(11784540676493656308)
XLA Ops:
  7.2 0.0 copy-start
  7.2 0.0 copy-start.1
  7.2 0.0 all-gather.2.cloned.1.call-start
  7.2 0.7 broadcast_compare_fusion
  8.0 0.7 copy.11
  8.7 0.6 reduce-window.6
  9.2 0.2 slice_reduce_fusion
  9.5 0.1 add_bitcast_fusion
  9.6 0.3 fusion.5
  9.8 0.0 copy-done
  9.8 0.3 multiply_reduce_fusion
  10.1 76.2 %psum.35 = f32[96]{0:T(128)S(1)} all-reduce(f32[96]{0:T(128)S(1)} %get-tuple-element.25), channel_id=1, replica_groups=mesh['section'=8,'vocab'=32] {'vocab'}, use_global_device_ids=true, to_apply=%region_4.5 | all-reduce | flops 96 | bytes 768 | tf_op jit(solution)/shard_map/psum | solution.py:27
  86.3 0.8 multiply_convert_fusion
  87.1 14.4 %all_gather.6 = bf16[768,256]{1,0:T(8,128)(2,1)} all-gather(bf16[96,256]{1,0:T(8,128)(2,1)S(1)} %multiply_convert_fusion), channel_id=1, replica_groups=mesh['section'=8,'vocab'=32] {'section'}, dimensions={0}, use_global_device_ids=true | all-gather | bytes 442368 | tf_op jit(solution)/shard_map/all_gather | solution.py:30
  101.5 0.0 all-gather.2.cloned.1.call-update
  101.5 0.0 reduce-scatter.3.cloned.1.call-start
  101.5 0.2 select_reduce_fusion
  101.8 0.1 broadcast_add_fusion
  101.9 0.1 add.110
  101.9 0.1 reshape.157
  102.1 0.0 copy-done.1
  102.1 0.0 copy-start.2
  102.1 4.5 gather_fusion
  106.6 0.0 copy-done.2
  106.6 0.7 fusion.30
  107.3 4.4 fusion.23
  111.7 110.2 %all-gather.2.cloned.1.call-done = bf16[768,8192]{1,0:T(8,128)(2,1)} async-done(((bf16[768,256]{1,0:T(8,128)(2,1)}), bf16[768,8192]{1,0:T(8,128)(2,1)}) %all-gather.2.cloned.1.call-update) | async-done | bytes 12582928 | tf_op jit(solution)/shard_map/all_gather | solution.py:35
  221.9 11.3 %fusion.31 = (f32[768]{0:T(1024)S(1)}, f32[768,384]{0,1:T(8,128)S(1)}) fusion(bf16[768,8192]{1,0:T(8,128)(2,1)} %all-gather.2.cloned.1.call-done, bf16[8192,384]{1,0:T(8,128)(2,1)} %param.8), kind=kOutput, calls=%fused_computation.66 | convolution fusion | flops 4832132096 | bytes 20057088 | tf_op jit(solution)/shard_map/dot_general | solution.py:38
  233.2 75.4 %pmax.7 = f32[768]{0:T(1024)S(1)} all-reduce(f32[768]{0:T(1024)S(1)} %get-tuple-element.27), channel_id=1, replica_groups=mesh['section'=8,'vocab'=32] {'section','vocab'}, use_global_device_ids=true, to_apply=%region_6.7 | all-reduce | flops 768 | bytes 6144 | tf_op jit(solution)/shard_map/pmax | solution.py:44
  308.6 0.3 fusion.1
  308.9 72.1 %all-reduce = (f32[768]{0:T(1024)S(1)}, f32[768]{0:T(1024)S(1)}) all-reduce(f32[768]{0:T(1024)S(1)} %get-tuple-element.5, f32[768]{0:T(1024)S(1)} %get-tuple-element.4), channel_id=1, replica_groups=mesh['section'=8,'vocab'=32] {'section','vocab'}, use_global_device_ids=true, to_apply=%region_8.9 | all-reduce | flops 1536 | bytes 12288 | tf_op jit(solution)/shard_map/psum | solution.py:46
  381.0 1.3 select_reduce_fusion.1
  382.3 12.6 %fusion = bf16[8192,768]{0,1:T(8,128)(2,1)} fusion(bf16[8192,384]{1,0:T(8,128)(2,1)} %param.8, f32[768,384]{0,1:T(8,128)S(1)} %get-tuple-element.28, f32[768]{0:T(1024)S(1)} %get-tuple-element.13, f32[768]{0:T(1024)S(1)} %get-tuple-element.16, s32[768]{0:T(1024)S(1)} %gather_fusion, s32[384]{0:T(512)S(1)} %iota_add_fusion), kind=kOutput, calls=%fused_computation.2 | convolution fusion | flops 4839899136 | bytes 20064768 | tf_op jit(solution)/shard_map/dot_general | solution.py:55
  394.9 0.0 reduce-scatter.3.cloned.1.call-update
  394.9 0.2 reduce-scatter.5.cloned.1.call-start
  395.8 231.7 %reduce-scatter.3.cloned.1.call-done = bf16[256,768]{0,1:T(8,128)(2,1)} async-done(((bf16[8192,768]{0,1:T(8,128)(2,1)}), bf16[256,768]{0,1:T(8,128)(2,1)}) %reduce-scatter.3.cloned.1.call-update) | async-done | bytes 393232 | tf_op jit(solution)/shard_map/reduce_scatter | solution.py:54
  627.5 0.0 reduce-scatter.5.cloned.1.call-update
  627.5 0.0 copy-start.3
  627.5 11.7 %convolution_convert_fusion.1 = bf16[8192,384]{1,0:T(8,128)(2,1)} fusion(bf16[768,8192]{1,0:T(8,128)(2,1)} %all-gather.2.cloned.1.call-done, f32[768,384]{0,1:T(8,128)S(1)} %get-tuple-element.28, f32[768]{0:T(1024)S(1)} %get-tuple-element.13, f32[768]{0:T(1024)S(1)} %get-tuple-element.16, s32[768]{0:T(1024)S(1)} %gather_fusion, s32[384]{0:T(512)S(1)} %iota_add_fusion), kind=kOutput, calls=%fused_computation.3 | convolution fusion | flops 4836753408 | bytes 20064768 | tf_op jit(solution)/shard_map/dot_general | solution.py:51
  639.2 22.3 %reduce-scatter.5.cloned.1.call-done = bf16[256,96]{0,1:T(8,128)(2,1)} async-done(((bf16[256,768]{0,1:T(8,128)(2,1)}), bf16[256,96]{0,1:T(8,128)(2,1)}) %reduce-scatter.5.cloned.1.call-update) | async-done | bytes 49168 | tf_op jit(solution)/shard_map/reduce_scatter | solution.py:62
  661.5 0.0 copy-done.3
  661.5 1.0 fusion.12
  662.5 13.7 %psum.39 = f32[256]{0:T(256)} all-reduce(f32[256]{0:T(256)S(1)} %get-tuple-element.6), channel_id=1, replica_groups=mesh['section'=8,'vocab'=32] {'section'}, use_global_device_ids=true, to_apply=%region_18.19 | all-reduce | flops 256 | bytes 2048 | tf_op jit(solution)/shard_map/psum | solution.py:72
  676.2 74.8 %psum.38 = f32[96]{0:T(128)S(1)} all-reduce(f32[96]{0:T(128)S(1)} %get-tuple-element.7), channel_id=1, replica_groups=mesh['section'=8,'vocab'=32] {'vocab'}, use_global_device_ids=true, to_apply=%region_16.17 | all-reduce | flops 96 | bytes 768 | tf_op jit(solution)/shard_map/psum | solution.py:67
  751.0 1.8 convolution_convert_fusion.2
  (10 shorter events, 0.1 us)
Async XLA Ops:
  7.2 2.7 copy-start
  7.2 94.9 %copy-start.1 = (s32[2048]{0:T(1024)S(1)}, s32[2048]{0:T(1024)}, u32[]{:S(2)}) copy-start(s32[2048]{0:T(1024)} %param.10) | copy-start | bytes 24580
  7.2 214.8 %all-gather.2.cloned.1.call-start = ((), (), s32[]{:S(2)}) async-start(), calls=%async_computation.2 | async-start | bytes 12976128 | tf_op jit(solution)/shard_map/all_gather | solution.py:35
  101.5 526.0 %reduce-scatter.3.cloned.1.call-start = ((), (), s32[]{:S(2)}) async-start(), calls=%async_computation.3 | async-start | bytes 12976128 | tf_op jit(solution)/shard_map/reduce_scatter | solution.py:54
  102.1 4.5 copy-start.2
  394.9 266.6 %reduce-scatter.5.cloned.1.call-start = ((), (), s32[]{:S(2)}) async-start(), calls=%async_computation.4 | async-start | bytes 442368 | tf_op jit(solution)/shard_map/reduce_scatter | solution.py:62
  627.5 34.0 %copy-start.3 = (f32[256]{0:T(256)S(1)}, f32[256]{0:T(256)}, u32[]{:S(2)}) copy-start(f32[256]{0:T(256)} %param.7) | copy-start | bytes 3076
Sparse Core Ops, SparseCore 0:
  101.6 120.2 all-gather.1
  395.0 232.4 reduce-scatter.2
  630.0 31.4 reduce-scatter.4
where the time goes:
time: 761 us; the launch traced here: 760 us
  waiting for transfers between devices  364 us (48%)
  blocking collectives  327 us (43%)
  matrix products  37.6 us (5%)
  between operations  15.7 us (2%)
  other arithmetic  9.79 us (1%)
    reduce_scatter x1, waiting for transfers between devices, body(): lax.psum_scatter(lax.dot_general(head_weight, dlogits, (((1,), (1,)), (()...  232 us
    all_gather x1, waiting for transfers between devices, body(): full_rows = lax.all_gather(section_rows, 'vocab', axis=1, tiled=True)  110 us
    psum x1, blocking collectives, body(): squares = lax.psum(jnp.sum(rows_own * rows_own, axis=1), 'vocab')  76.2 us
    pmax x1, blocking collectives, body(): row_peak = lax.pmax(local_peak, ('section', 'vocab'))  75.4 us
    psum x1, blocking collectives, body(): inner_dots = lax.psum(jnp.sum(scaled * rows_own, axis=1), 'vocab') / D  74.8 us
    psum x1, blocking collectives, body(): lax.psum((local_total, picked_part), ('section', 'vocab'))  72.1 us
    reduce_scatter x1, waiting for transfers between devices, body(): lax.psum_scatter(grads_turned, 'section', scatter_dimension=1, tiled=True)  22.3 us
  transfers between devices with their start and end apart: 3, of which 3 were waited for; matrix products, arithmetic and copies ran while one was open for 3% of the time, Pallas kernels for 0%

commit v1 on v0

--- a/solution.py
+++ b/solution.py
@@ -64,7 +64,7 @@
     )
     d_normed = own_grads.T
     scaled = d_normed * norm_gain[None, :]
-    inner_dots = lax.psum(jnp.sum(scaled * rows_own, axis=1), "vocab") / D
+    inner_dots = jnp.sum(lax.all_gather(jnp.sum(scaled * rows_own, axis=1), "vocab"), axis=0) / D
     d_rows = (
         inverse[:, None] * scaled - rows_own * (inverse * inverse * inverse * inner_dots)[:, None]
     )

time: 761 us -> 830 us (1.091)
  blocking collectives: 327 us -> 395 us
    unnamed x0 -> x1, blocking collectives: none -> 143 us
    psum x1 -> x0, blocking collectives: 74.8 us -> none  [body(): inner_dots = lax.psum(jnp.sum(scaled * rows_own, axis=1), 'vocab') / D]
where the time goes in v1:
time: 830 us; the launch traced here: 829 us
  blocking collectives  395 us (48%)
  waiting for transfers between devices  363 us (44%)
  matrix products  37.6 us (5%)
  between operations  16.3 us (2%)
  other arithmetic  9.82 us (1%)
    reduce_scatter x1, waiting for transfers between devices, body(): lax.psum_scatter(lax.dot_general(head_weight, dlogits, (((1,), (1,)), (()...  230 us
    unnamed x1, blocking collectives  143 us
    all_gather x1, waiting for transfers between devices, body(): full_rows = lax.all_gather(section_rows, 'vocab', axis=1, tiled=True)  110 us
    psum x1, blocking collectives, body(): squares = lax.psum(jnp.sum(rows_own * rows_own, axis=1), 'vocab')  76.2 us
    pmax x1, blocking collectives, body(): row_peak = lax.pmax(local_peak, ('section', 'vocab'))  75.4 us
    psum x1, blocking collectives, body(): lax.psum((local_total, picked_part), ('section', 'vocab'))  72.1 us
    reduce_scatter x1, waiting for transfers between devices, body(): lax.psum_scatter(grads_turned, 'section', scatter_dimension=1, tiled=True)  22.6 us
  transfers between devices with their start and end apart: 3, of which 3 were waited for; matrix products, arithmetic and copies ran while one was open for 3% of the time, Pallas kernels for 0%

profile of v1, /device:TPU:0, one launch (start us, length us, event | category | flops | bytes accessed | tf_op | source)
XLA Modules:
  0.0 828.9 jit_solution(13097771108199394185)
XLA Ops:
  7.2 0.0 copy-start
  7.2 0.0 copy-start.1
  7.2 0.0 all-gather.3.cloned.1.call-start
  7.2 0.7 broadcast_compare_fusion
  8.0 0.7 copy.11
  8.7 0.6 reduce-window.6
  9.2 0.2 slice_reduce_fusion
  9.5 0.1 add_bitcast_fusion
  9.6 0.3 fusion.5
  9.8 0.0 copy-done
  9.8 0.3 multiply_reduce_fusion
  10.1 76.2 %psum.28 = f32[96]{0:T(128)S(1)} all-reduce(f32[96]{0:T(128)S(1)} %get-tuple-element.25), channel_id=1, replica_groups=mesh['section'=8,'vocab'=32] {'vocab'}, use_global_device_ids=true, to_apply=%region_4.5 | all-reduce | flops 96 | bytes 768 | tf_op jit(solution)/shard_map/psum | solution.py:27
  86.3 0.8 multiply_convert_fusion
  87.1 14.4 %all_gather.12 = bf16[768,256]{1,0:T(8,128)(2,1)} all-gather(bf16[96,256]{1,0:T(8,128)(2,1)S(1)} %multiply_convert_fusion), channel_id=1, replica_groups=mesh['section'=8,'vocab'=32] {'section'}, dimensions={0}, use_global_device_ids=true | all-gather | bytes 442368 | tf_op jit(solution)/shard_map/all_gather | solution.py:30
  101.5 0.0 all-gather.3.cloned.1.call-update
  101.5 0.0 reduce-scatter.3.cloned.1.call-start
  101.5 0.2 select_reduce_fusion
  101.8 0.1 broadcast_add_fusion
  101.9 0.1 add.108
  101.9 0.1 reshape.157
  102.1 0.0 copy-done.1
  102.1 0.0 copy-start.2
  102.1 4.5 gather_fusion
  106.6 0.0 copy-done.2
  106.6 0.7 fusion.30
  107.3 4.4 fusion.23
  111.7 110.2 %all-gather.3.cloned.1.call-done = bf16[768,8192]{1,0:T(8,128)(2,1)} async-done(((bf16[768,256]{1,0:T(8,128)(2,1)}), bf16[768,8192]{1,0:T(8,128)(2,1)}) %all-gather.3.cloned.1.call-update) | async-done | bytes 12582928 | tf_op jit(solution)/shard_map/all_gather | solution.py:35
  221.9 11.3 %fusion.31 = (f32[768]{0:T(1024)S(1)}, f32[768,384]{0,1:T(8,128)S(1)}) fusion(bf16[768,8192]{1,0:T(8,128)(2,1)} %all-gather.3.cloned.1.call-done, bf16[8192,384]{1,0:T(8,128)(2,1)} %param.8), kind=kOutput, calls=%fused_computation.66 | convolution fusion | flops 4832132096 | bytes 20057088 | tf_op jit(solution)/shard_map/dot_general | solution.py:38
  233.2 75.4 %pmax.7 = f32[768]{0:T(1024)S(1)} all-reduce(f32[768]{0:T(1024)S(1)} %get-tuple-element.27), channel_id=1, replica_groups=mesh['section'=8,'vocab'=32] {'section','vocab'}, use_global_device_ids=true, to_apply=%region_6.7 | all-reduce | flops 768 | bytes 6144 | tf_op jit(solution)/shard_map/pmax | solution.py:44
  308.6 0.3 fusion.1
  308.9 72.1 %all-reduce.1 = (f32[768]{0:T(1024)S(1)}, f32[768]{0:T(1024)S(1)}) all-reduce(f32[768]{0:T(1024)S(1)} %get-tuple-element.5, f32[768]{0:T(1024)S(1)} %get-tuple-element.4), channel_id=1, replica_groups=mesh['section'=8,'vocab'=32] {'section','vocab'}, use_global_device_ids=true, to_apply=%region_8.9 | all-reduce | flops 1536 | bytes 12288 | tf_op jit(solution)/shard_map/psum | solution.py:46
  381.0 1.3 select_reduce_fusion.1
  382.3 12.6 %fusion = bf16[8192,768]{0,1:T(8,128)(2,1)} fusion(bf16[8192,384]{1,0:T(8,128)(2,1)} %param.8, f32[768,384]{0,1:T(8,128)S(1)} %get-tuple-element.28, f32[768]{0:T(1024)S(1)} %get-tuple-element.13, f32[768]{0:T(1024)S(1)} %get-tuple-element.16, s32[768]{0:T(1024)S(1)} %gather_fusion, s32[384]{0:T(512)S(1)} %iota_add_fusion), kind=kOutput, calls=%fused_computation.2 | convolution fusion | flops 4839899136 | bytes 20064768 | tf_op jit(solution)/shard_map/dot_general | solution.py:55
  394.9 0.0 copy-start.4
  394.9 0.0 reduce-scatter.3.cloned.1.call-update
  394.9 0.2 reduce-scatter.5.cloned.1.call-start
  395.1 0.4 copy-done.4
  395.6 0.6 dynamic-slice
  397.4 229.9 %reduce-scatter.3.cloned.1.call-done = bf16[256,768]{0,1:T(8,128)(2,1)} async-done(((bf16[8192,768]{0,1:T(8,128)(2,1)}), bf16[256,768]{0,1:T(8,128)(2,1)}) %reduce-scatter.3.cloned.1.call-update) | async-done | bytes 393232 | tf_op jit(solution)/shard_map/reduce_scatter | solution.py:54
  627.3 0.0 reduce-scatter.5.cloned.1.call-update
  627.4 0.0 copy-start.3
  627.4 11.7 %convolution_convert_fusion.1 = bf16[8192,384]{1,0:T(8,128)(2,1)} fusion(bf16[768,8192]{1,0:T(8,128)(2,1)} %all-gather.3.cloned.1.call-done, f32[768,384]{0,1:T(8,128)S(1)} %get-tuple-element.28, f32[768]{0:T(1024)S(1)} %get-tuple-element.13, f32[768]{0:T(1024)S(1)} %get-tuple-element.16, s32[768]{0:T(1024)S(1)} %gather_fusion, s32[384]{0:T(512)S(1)} %iota_add_fusion), kind=kOutput, calls=%fused_computation.3 | convolution fusion | flops 4836753408 | bytes 20064768 | tf_op jit(solution)/shard_map/dot_general | solution.py:51
  639.1 22.6 %reduce-scatter.5.cloned.1.call-done = bf16[256,96]{0,1:T(8,128)(2,1)} async-done(((bf16[256,768]{0,1:T(8,128)(2,1)}), bf16[256,96]{0,1:T(8,128)(2,1)}) %reduce-scatter.5.cloned.1.call-update) | async-done | bytes 49168 | tf_op jit(solution)/shard_map/reduce_scatter | solution.py:62
  661.6 0.0 copy-done.3
  661.6 1.0 fusion.12
  662.6 13.6 %psum.31 = f32[256]{0:T(256)} all-reduce(f32[256]{0:T(256)S(1)} %get-tuple-element.6), channel_id=1, replica_groups=mesh['section'=8,'vocab'=32] {'section'}, use_global_device_ids=true, to_apply=%region_18.19 | all-reduce | flops 256 | bytes 2048 | tf_op jit(solution)/shard_map/psum | solution.py:72
  676.3 0.2 dynamic-update-slice
  676.5 142.8 %all-reduce = f32[3072]{0:T(1024)S(1)} all-reduce(f32[3072]{0:T(1024)S(1)} %dynamic-update-slice), channel_id=2, replica_groups=mesh['section'=8,'vocab'=32] {'vocab'}, use_global_device_ids=true, to_apply=%add | all-reduce | flops 3072 | bytes 24576
  819.3 0.1 reshape.181
  819.4 1.8 convolution_convert_fusion.2
  (12 shorter events, 0.2 us)
Async XLA Ops:
  7.2 2.7 copy-start
  7.2 94.9 %copy-start.1 = (s32[2048]{0:T(1024)S(1)}, s32[2048]{0:T(1024)}, u32[]{:S(2)}) copy-start(s32[2048]{0:T(1024)} %param.10) | copy-start | bytes 24580
  7.2 214.8 %all-gather.3.cloned.1.call-start = ((), (), s32[]{:S(2)}) async-start(), calls=%async_computation.2 | async-start | bytes 12976128 | tf_op jit(solution)/shard_map/all_gather | solution.py:35
  101.5 525.9 %reduce-scatter.3.cloned.1.call-start = ((), (), s32[]{:S(2)}) async-start(), calls=%async_computation.3 | async-start | bytes 12976128 | tf_op jit(solution)/shard_map/reduce_scatter | solution.py:54
  102.1 4.5 copy-start.2
  394.9 0.7 copy-start.4
  394.9 266.7 %reduce-scatter.5.cloned.1.call-start = ((), (), s32[]{:S(2)}) async-start(), calls=%async_computation.4 | async-start | bytes 442368 | tf_op jit(solution)/shard_map/reduce_scatter | solution.py:62
  627.4 34.3 %copy-start.3 = (f32[256]{0:T(256)S(1)}, f32[256]{0:T(256)}, u32[]{:S(2)}) copy-start(f32[256]{0:T(256)} %param.7) | copy-start | bytes 3076
Sparse Core Ops, SparseCore 0:
  101.6 120.2 all-gather.2
  395.0 232.2 reduce-scatter.2
  629.9 31.7 reduce-scatter.4
